TPU v7x, 32 devices: a whole 2x2x4 slice. The times are simulated.
32 devices in a mesh: task: 4 (over y, x), batch: 8 (over z, core).
Axes of the slice: x: 2, y: 2, z: 4, core: 2. Of those that a mesh axis runs over, the one named last changes fastest.
Arguments:
- tokens: bfloat16 [32768, 1024], P(('task', 'batch')), may hold values from -6 to 6
- lengths: int32 [32, 4], P(('task', 'batch')), may hold values from 0 to 1024, as said below
- task_ids: int32 [32, 4], replicated, may hold values from 0 to 63, as said below
- prefix_embed: bfloat16 [64, 10, 1024], P('task', None, 'batch'), may hold values from -6 to 6
- reparam_inner: bfloat16 [64, 1024, 512], P('task', 'batch'), may hold values from -0.1875 to 0.1875
- reparam_inner_bias: bfloat16 [64, 512], P('task'), may hold values from -3 to 3
- reparam_outer: bfloat16 [64, 512, 2048], P('task', None, 'batch'), may hold values from -0.4375 to 0.4375
- reparam_outer_bias: bfloat16 [64, 2048], P('task', 'batch'), may hold values from -3 to 3
- first_gain: bfloat16 [1024], replicated, may hold values from 0.5 to 1.5
- first_bias: bfloat16 [1024], replicated, may hold values from -3 to 3
- input_weight: bfloat16 [1024, 3072], replicated, may hold values from -0.1875 to 0.1875
- output_weight: bfloat16 [1024, 1024], replicated, may hold values from -1.5 to 1.5
- second_gain: bfloat16 [1024], replicated, may hold values from 0.5 to 1.5
- second_bias: bfloat16 [1024], replicated, may hold values from -3 to 3
- expand_weight: bfloat16 [1024, 4096], replicated, may hold values from -0.1875 to 0.1875
- contract_weight: bfloat16 [4096, 1024], replicated, may hold values from -0.09375 to 0.09375
- output_cotangent: bfloat16 [32768, 1024], P(('task', 'batch')), may hold values from -6 to 6
Outputs:
- output: bfloat16 [32768, 1024], P(('task', 'batch'))
- input_grad: bfloat16 [32768, 1024], P(('task', 'batch'))
- grad_embed: float32 [64, 10, 1024], P('task', None, 'batch')
- grad_inner: float32 [64, 1024, 512], P('task', 'batch')
- grad_inner_bias: float32 [64, 512], P('task')
- grad_outer: float32 [64, 512, 2048], P('task', None, 'batch')
- grad_outer_bias: float32 [64, 2048], P('task', 'batch')
Inputs may be any that keep to these rules, and one draw needn't show every extreme that they name: `task_ids`: the 4 examples of one device have tasks t with 4 different values of t // 16. Each device's row is either 1024 followed by zeros (one sequence) or 4 lengths of 256; both kinds occur in every draw.
All inputs are finite; a program needn't handle non-finite values.
Results may differ from a plain program's by a relative error of at most 0.013.
Values may be sent and summed in bfloat16 or wider, within the bound.
A program may use at most 256 MiB of HBM per device.

v0:
```python
import jax
import jax.numpy as jnp
from jax import lax
from jax.sharding import PartitionSpec as P

HEADS = 16


def layer_norm(values, norm_gain, norm_bias):
    average = jnp.mean(values, axis=-1, keepdims=True)
    centered = values - average
    variance = jnp.mean(centered * centered, axis=-1, keepdims=True)
    return centered * lax.rsqrt(variance + 1e-05) * norm_gain + norm_bias


def gelu_tanh(values):
    return (
        0.5
        * values
        * (1.0 + jnp.tanh(0.7978845608028654 * (values + 0.044715 * values * values * values)))
    )


def build_visible(lengths_row, row_count, prefix_len):
    slot_ends = jnp.cumsum(lengths_row)
    positions = jnp.arange(row_count, dtype=jnp.int32)
    segment = jnp.sum((positions[:, None] >= slot_ends[None, :]).astype(jnp.int32), axis=1)
    prefix_slot = jnp.arange(lengths_row.shape[0] * prefix_len, dtype=jnp.int32) // prefix_len
    prefix_seen = segment[:, None] == prefix_slot[None, :]
    token_seen = (segment[:, None] == segment[None, :]) & (positions[None, :] <= positions[:, None])
    return jnp.concatenate([prefix_seen, token_seen], axis=1)


def split_groups(matrix, groups):
    item_count = matrix.shape[0]
    return matrix.reshape(item_count, groups, matrix.shape[1] // groups).transpose(1, 0, 2)


def merge_groups(stacked):
    return stacked.transpose(1, 0, 2).reshape(stacked.shape[1], stacked.shape[0] * stacked.shape[2])


def pick_sum(selector, values):
    return jnp.sum(jnp.where(selector[:, :, None], values[:, None, :], 0.0), axis=0)


def local(
    tokens,
    lengths,
    task_ids,
    prefix_embed,
    reparam_inner,
    reparam_inner_bias,
    reparam_outer,
    reparam_outer_bias,
    first_gain,
    first_bias,
    input_weight,
    output_weight,
    second_gain,
    second_bias,
    expand_weight,
    contract_weight,
    output_cotangent,
):
    row_count = tokens.shape[0]
    width = tokens.shape[1]
    task_dev = prefix_embed.shape[0]
    prefix_len = prefix_embed.shape[1]
    slot_count = lengths.shape[1]
    head_dim = width // HEADS
    scale = head_dim ** (-0.5)
    group_heads = min(HEADS, 4)
    groups = HEADS // group_heads
    group_width = group_heads * head_dim
    task_count = lax.axis_size("task")
    batch_count = lax.axis_size("batch")
    device_count = task_count * batch_count
    pair_cols = reparam_outer.shape[2]
    task_row = lax.axis_index("task")
    device_pos = lax.axis_index(("task", "batch"))
    owner_rows = task_ids // task_dev
    row_match = owner_rows[:, :, None] == jnp.arange(task_count, dtype=jnp.int32)[None, None, :]
    row_task = jnp.sum(jnp.where(row_match, task_ids[:, :, None], 0), axis=1)
    own_tasks = task_row * task_dev + jnp.arange(task_dev, dtype=jnp.int32)
    partner_tasks = jnp.take(row_task, task_row, axis=1)
    partner_pick = partner_tasks[:, None] == own_tasks[None, :]
    pre_part = jnp.einsum(
        "tpd,tdh->tph", prefix_embed, reparam_inner, preferred_element_type=jnp.float32
    )
    pre_sum = lax.psum(pre_part, "batch")
    hidden_full = jnp.tanh(pre_sum + reparam_inner_bias.astype(jnp.float32)[:, None, :])
    hidden_low = hidden_full.astype(jnp.bfloat16)
    kv_cols = (
        jnp.einsum("tph,thc->tpc", hidden_low, reparam_outer, preferred_element_type=jnp.float32)
        + reparam_outer_bias.astype(jnp.float32)[:, None, :]
    ).astype(jnp.bfloat16)
    outgoing = jnp.einsum(
        "et,tpc->epc",
        partner_pick.astype(jnp.bfloat16),
        kv_cols,
        preferred_element_type=jnp.float32,
    ).astype(jnp.bfloat16)
    incoming = lax.all_to_all(
        outgoing.reshape(device_count, prefix_len * pair_cols),
        ("task", "batch"),
        split_axis=0,
        concat_axis=0,
        tiled=True,
    )
    by_row = (
        incoming.reshape(task_count, batch_count, prefix_len, pair_cols)
        .transpose(0, 2, 1, 3)
        .reshape(task_count, prefix_len * 2 * width)
    )
    own_owner = jnp.take(owner_rows, device_pos, axis=0)
    slot_match = own_owner[:, None] == jnp.arange(task_count, dtype=jnp.int32)[None, :]
    slot_pick = slot_match.astype(jnp.bfloat16)
    prefix_kv = (
        jnp.dot(slot_pick, by_row, preferred_element_type=jnp.float32)
        .astype(jnp.bfloat16)
        .reshape(slot_count, prefix_len, 2 * width)
    )
    gain_one = first_gain.astype(jnp.float32)
    bias_one = first_bias.astype(jnp.float32)
    gain_two = second_gain.astype(jnp.float32)
    bias_two = second_bias.astype(jnp.float32)
    residual_in = tokens.astype(jnp.float32)
    normed = layer_norm(residual_in, gain_one, bias_one).astype(jnp.bfloat16)
    projected = jnp.dot(normed, input_weight, preferred_element_type=jnp.float32).astype(
        jnp.bfloat16
    )
    queries = projected[:, :width]
    keys_all = jnp.concatenate(
        [
            prefix_kv[:, :, :width].reshape(slot_count * prefix_len, width),
            projected[:, width : 2 * width],
        ],
        axis=0,
    )
    values_all = jnp.concatenate(
        [
            prefix_kv[:, :, width:].reshape(slot_count * prefix_len, width),
            projected[:, 2 * width :],
        ],
        axis=0,
    )
    key_count = keys_all.shape[0]
    visible = build_visible(lengths[0], row_count, prefix_len)
    query_groups = split_groups(queries, groups)
    key_groups = split_groups(keys_all, groups)
    value_groups = split_groups(values_all, groups)

    def group_scores(group_query, group_key):
        query_heads = group_query.reshape(row_count, group_heads, head_dim)
        key_heads = group_key.reshape(key_count, group_heads, head_dim)
        raw_scores = (
            jnp.einsum("qhd,khd->hqk", query_heads, key_heads, preferred_element_type=jnp.float32)
            * scale
        )
        return jnp.where(visible[None], raw_scores, -1e30)

    def attend(carry, group_parts):
        group_query, group_key, group_value = group_parts
        scores = group_scores(group_query, group_key)
        top_score = jnp.max(scores, axis=-1, keepdims=True)
        lifted = jnp.exp(scores - top_score)
        total = jnp.sum(lifted, axis=-1, keepdims=True)
        probs = lifted / total
        value_heads = group_value.reshape(key_count, group_heads, head_dim)
        mixed = jnp.einsum(
            "hqk,khd->qhd",
            probs.astype(jnp.bfloat16),
            value_heads,
            preferred_element_type=jnp.float32,
        )
        return (
            carry,
            (mixed.reshape(row_count, group_width), (top_score + jnp.log(total))[..., 0]),
        )

    unused_carry, (mixed_groups, log_totals) = lax.scan(
        attend, jnp.float32(0.0), (query_groups, key_groups, value_groups)
    )
    attended = merge_groups(mixed_groups).astype(jnp.bfloat16)
    mid = residual_in + jnp.dot(attended, output_weight, preferred_element_type=jnp.float32)
    normed_two = layer_norm(mid, gain_two, bias_two).astype(jnp.bfloat16)
    hidden_pre = jnp.dot(normed_two, expand_weight, preferred_element_type=jnp.float32)
    activated = gelu_tanh(hidden_pre).astype(jnp.bfloat16)
    output = (mid + jnp.dot(activated, contract_weight, preferred_element_type=jnp.float32)).astype(
        jnp.bfloat16
    )
    grad_act = jnp.einsum(
        "rc,fc->rf", output_cotangent, contract_weight, preferred_element_type=jnp.float32
    )
    unused_gelu, gelu_pull = jax.vjp(gelu_tanh, hidden_pre)
    grad_hidden = gelu_pull(grad_act)[0].astype(jnp.bfloat16)
    grad_normed_two = jnp.einsum(
        "rf,cf->rc", grad_hidden, expand_weight, preferred_element_type=jnp.float32
    )
    unused_norm_two, norm_two_pull = jax.vjp(
        lambda values: layer_norm(values, gain_two, bias_two), mid
    )
    grad_mid = output_cotangent.astype(jnp.float32) + norm_two_pull(grad_normed_two)[0]
    grad_mid_low = grad_mid.astype(jnp.bfloat16)
    grad_attended = jnp.einsum(
        "rc,dc->rd", grad_mid_low, output_weight, preferred_element_type=jnp.float32
    ).astype(jnp.bfloat16)
    grad_groups = split_groups(grad_attended, groups)

    def attend_back(carry, group_parts):
        group_query, group_key, group_value, group_total, group_grad = group_parts
        scores = group_scores(group_query, group_key)
        probs = jnp.exp(scores - group_total[..., None])
        query_heads = group_query.reshape(row_count, group_heads, head_dim)
        key_heads = group_key.reshape(key_count, group_heads, head_dim)
        value_heads = group_value.reshape(key_count, group_heads, head_dim)
        grad_heads = group_grad.reshape(row_count, group_heads, head_dim)
        grad_probs = jnp.einsum(
            "qhd,khd->hqk", grad_heads, value_heads, preferred_element_type=jnp.float32
        )
        inner_sum = jnp.sum(probs * grad_probs, axis=-1, keepdims=True)
        grad_scores = (probs * (grad_probs - inner_sum)).astype(jnp.bfloat16)
        grad_query = (
            jnp.einsum("hqk,khd->qhd", grad_scores, key_heads, preferred_element_type=jnp.float32)
            * scale
        )
        grad_key = (
            jnp.einsum("hqk,qhd->khd", grad_scores, query_heads, preferred_element_type=jnp.float32)
            * scale
        )
        grad_value = jnp.einsum(
            "hqk,qhd->khd",
            probs.astype(jnp.bfloat16),
            grad_heads,
            preferred_element_type=jnp.float32,
        )
        return (
            carry,
            (
                grad_query.reshape(row_count, group_width),
                grad_key.reshape(key_count, group_width),
                grad_value.reshape(key_count, group_width),
            ),
        )

    unused_back, (grad_query_groups, grad_key_groups, grad_value_groups) = lax.scan(
        attend_back,
        jnp.float32(0.0),
        (query_groups, key_groups, value_groups, log_totals, grad_groups),
    )
    grad_keys_all = merge_groups(grad_key_groups)
    grad_values_all = merge_groups(grad_value_groups)
    prefix_rows = slot_count * prefix_len
    grad_qkv = jnp.concatenate(
        [
            merge_groups(grad_query_groups),
            grad_keys_all[prefix_rows:],
            grad_values_all[prefix_rows:],
        ],
        axis=1,
    ).astype(jnp.bfloat16)
    grad_normed = jnp.einsum(
        "rk,dk->rd", grad_qkv, input_weight, preferred_element_type=jnp.float32
    )
    unused_norm_one, norm_one_pull = jax.vjp(
        lambda values: layer_norm(values, gain_one, bias_one), residual_in
    )
    input_grad = (grad_mid + norm_one_pull(grad_normed)[0]).astype(jnp.bfloat16)
    grad_prefix = jnp.concatenate(
        [
            grad_keys_all[:prefix_rows].reshape(slot_count, prefix_len, width),
            grad_values_all[:prefix_rows].reshape(slot_count, prefix_len, width),
        ],
        axis=2,
    ).reshape(slot_count, prefix_len * 2 * width)
    by_owner = pick_sum(slot_match, grad_prefix)
    outgoing_grad = (
        by_owner.reshape(task_count, prefix_len, batch_count, pair_cols)
        .transpose(0, 2, 1, 3)
        .reshape(device_count, prefix_len * pair_cols)
    )
    incoming_grad = lax.all_to_all(
        outgoing_grad, ("task", "batch"), split_axis=0, concat_axis=0, tiled=True
    )
    grad_cols = pick_sum(partner_pick, incoming_grad).reshape(task_dev, prefix_len, pair_cols)
    grad_table_low = grad_cols.astype(jnp.bfloat16)
    grad_outer_bias = jnp.sum(grad_table_low.astype(jnp.float32), axis=1)
    grad_outer = jnp.einsum(
        "tph,tpc->thc", hidden_low, grad_table_low, preferred_element_type=jnp.float32
    )
    grad_hidden_part = jnp.einsum(
        "tpc,thc->tph", grad_table_low, reparam_outer, preferred_element_type=jnp.float32
    )
    grad_hidden_table = lax.psum(grad_hidden_part, "batch")
    grad_pre = (grad_hidden_table * (1.0 - hidden_full * hidden_full)).astype(jnp.bfloat16)
    grad_inner_bias = jnp.sum(grad_pre.astype(jnp.float32), axis=1)
    grad_inner = jnp.einsum(
        "tpd,tph->tdh", prefix_embed, grad_pre, preferred_element_type=jnp.float32
    )
    grad_embed = jnp.einsum(
        "tph,tdh->tpd", grad_pre, reparam_inner, preferred_element_type=jnp.float32
    )
    return (
        output,
        input_grad,
        grad_embed,
        grad_inner,
        grad_inner_bias,
        grad_outer,
        grad_outer_bias,
    )


def solution(mesh):
    placed = (
        P(("task", "batch"), None),
        P(("task", "batch"), None),
        P(),
        P("task", None, "batch"),
        P("task", "batch", None),
        P("task", None),
        P("task", None, "batch"),
        P("task", "batch"),
        P(),
        P(),
        P(),
        P(),
        P(),
        P(),
        P(),
        P(),
        P(("task", "batch"), None),
    )
    return jax.shard_map(
        local,
        mesh=mesh,
        in_specs=placed,
        out_specs=(
            P(("task", "batch"), None),
            P(("task", "batch"), None),
            P("task", None, "batch"),
            P("task", "batch", None),
            P("task", None),
            P("task", None, "batch"),
            P("task", "batch"),
        ),
        check_vma=False,
    )
```

profile of v0, /device:TPU:0, one launch (start us, length us, event | category | flops | bytes accessed | tf_op | source)
XLA Modules:
  0.0 655.3 jit_solution(17415428479053290672)
XLA Ops:
  7.2 2.9 fusion.55
  10.2 3.9 copy.108
  19.7 10.3 %convolution_convert_fusion.1 = bf16[1024,3072]{1,0:T(8,128)(2,1)S(1)} fusion(bf16[1024,3072]{1,0:T(8,128)(2,1)} %param.31, bf16[1024,1024]{0,1:T(8,128)(2,1)S(1)} %copy-done.2, f32[1024]{0:T(1024)S(1)} %convert_element_type.110, f32[1024]{0:T(1024)S(1)} %convert_element_type.109, f32[1024]{0:T(1024)S(1)} %fusion.61, f32[1024]{0:T(1024)S(1)} %broadcast_multiply_fusion.1), kind=kOutput, calls=%fused_computation.58 | convolution fusion | flops 6451888128 | bytes 14696448 | tf_op jit(solution)/shard_map/dot_general | solution.py:130
  30.1 2.9 fusion.77
  36.6 32.6 %all-reduce.3.cloned.1.call-done = f32[16,10,512]{2,1,0:T(8,128)} async-done(((f32[16,10,512]{2,1,0:T(8,128)}), f32[16,10,512]{2,1,0:T(8,128)}) %all-reduce.3.cloned.1.call-update) | async-done | bytes 327696 | tf_op jit(solution)/shard_map/psum | solution.py:91
  69.2 3.0 fusion.50
  75.3 2.3 reduce.2
  79.2 3.9 all-to-all-start
  83.2 4.0 copy.131
  87.1 4.0 copy.133
  91.1 3.9 copy.132
  96.2 3.9 copy.120
  108.9 5.3 maximum_bitcast_fusion
  115.7 117.9 %while.28 = (s32[]{:T(128)}, bf16[4,1024,256]{1,2,0:T(8,128)(2,1)}, f32[4,4,1024]{2,1,0:T(4,128)S(1)}, bf16[4,1064,256]{1,2,0:T(8,128)(2,1)}, pred[1024,1064]{0,...) while((s32[]{:T(128)}, bf16[4,1024,256]{1,2,0:T(8,128)(2,1)}, ...), condition=%wide.region_9.10_spmd, body=%wide.region_6.9_spmd.sunk | while | flops 1150545920 | bytes 59932780 | solution.py:182
  119.0 7.7 %fusion.145 = (f32[4,1024]{1,0:T(4,128)S(1)}, f32[4,1024,1064]{1,2,0:T(8,128)}) fusion(bf16[1024,4,64]{0,2,1:T(8,128)(2,1)S(1)} %bitcast.173, bf16[1064,4,64]{0,2,1:T(8,128)(2,1)S(1)} %bitcast.171, pred[1024,1064]{0,1:T(8,128)(4,1)S(1)} %get-tuple-element.360), kind=kOutput, calls=%fused_computation.153.clone.1 | convolution fusion | flops 570912768 | bytes 19607552 | tf_op jit(solution)/shard_map/while/body/eval_jaxpr/qhd,khd->hqk/dot_general | solution.py:158
  126.7 8.3 %fusion.146 = f32[4,1024]{1,0:T(4,128)S(1)} fusion(f32[4,1024,1064]{1,2,0:T(8,128)} %get-tuple-element.324, f32[4,1024]{1,0:T(4,128)S(1)} %get-tuple-element.325), kind=kLoop, calls=%fused_computation.4.clone.1 | loop fusion | flops 8712192 | bytes 17465344 | tf_op jit(solution)/shard_map/while/body/eval_jaxpr/reduce_sum | solution.py:168
  134.9 9.3 %fusion.147 = bf16[4,64,1024]{2,1,0:T(8,128)(2,1)S(1)} fusion(bf16[1064,4,64]{0,2,1:T(8,128)(2,1)} %bitcast.176, f32[4,1024,1064]{1,2,0:T(8,128)} %get-tuple-element.324, f32[4,1024]{1,0:T(4,128)S(1)} %fusion.146, f32[4,1024]{1,0:T(4,128)S(1)} %get-tuple-element.325), kind=kOutput, calls=%fused_computation.5.clone.1 | convolution fusion | flops 570916864 | bytes 18534400 | tf_op jit(solution)/shard_map/while/body/eval_jaxpr/hqk,khd->qhd/dot_general | solution.py:171
  148.3 7.7 %fusion.145 = (f32[4,1024]{1,0:T(4,128)S(1)}, f32[4,1024,1064]{1,2,0:T(8,128)}) fusion(bf16[1024,4,64]{0,2,1:T(8,128)(2,1)S(1)} %bitcast.173, bf16[1064,4,64]{0,2,1:T(8,128)(2,1)S(1)} %bitcast.171, pred[1024,1064]{0,1:T(8,128)(4,1)S(1)} %get-tuple-element.360), kind=kOutput, calls=%fused_computation.153.clone.1 | convolution fusion | flops 570912768 | bytes 19607552 | tf_op jit(solution)/shard_map/while/body/eval_jaxpr/qhd,khd->hqk/dot_general | solution.py:158
  156.0 8.3 %fusion.146 = f32[4,1024]{1,0:T(4,128)S(1)} fusion(f32[4,1024,1064]{1,2,0:T(8,128)} %get-tuple-element.324, f32[4,1024]{1,0:T(4,128)S(1)} %get-tuple-element.325), kind=kLoop, calls=%fused_computation.4.clone.1 | loop fusion | flops 8712192 | bytes 17465344 | tf_op jit(solution)/shard_map/while/body/eval_jaxpr/reduce_sum | solution.py:168
  164.3 9.3 %fusion.147 = bf16[4,64,1024]{2,1,0:T(8,128)(2,1)S(1)} fusion(bf16[1064,4,64]{0,2,1:T(8,128)(2,1)} %bitcast.176, f32[4,1024,1064]{1,2,0:T(8,128)} %get-tuple-element.324, f32[4,1024]{1,0:T(4,128)S(1)} %fusion.146, f32[4,1024]{1,0:T(4,128)S(1)} %get-tuple-element.325), kind=kOutput, calls=%fused_computation.5.clone.1 | convolution fusion | flops 570916864 | bytes 18534400 | tf_op jit(solution)/shard_map/while/body/eval_jaxpr/hqk,khd->qhd/dot_general | solution.py:171
  177.7 7.7 %fusion.145 = (f32[4,1024]{1,0:T(4,128)S(1)}, f32[4,1024,1064]{1,2,0:T(8,128)}) fusion(bf16[1024,4,64]{0,2,1:T(8,128)(2,1)S(1)} %bitcast.173, bf16[1064,4,64]{0,2,1:T(8,128)(2,1)S(1)} %bitcast.171, pred[1024,1064]{0,1:T(8,128)(4,1)S(1)} %get-tuple-element.360), kind=kOutput, calls=%fused_computation.153.clone.1 | convolution fusion | flops 570912768 | bytes 19607552 | tf_op jit(solution)/shard_map/while/body/eval_jaxpr/qhd,khd->hqk/dot_general | solution.py:158
  185.4 8.3 %fusion.146 = f32[4,1024]{1,0:T(4,128)S(1)} fusion(f32[4,1024,1064]{1,2,0:T(8,128)} %get-tuple-element.324, f32[4,1024]{1,0:T(4,128)S(1)} %get-tuple-element.325), kind=kLoop, calls=%fused_computation.4.clone.1 | loop fusion | flops 8712192 | bytes 17465344 | tf_op jit(solution)/shard_map/while/body/eval_jaxpr/reduce_sum | solution.py:168
  193.7 9.3 %fusion.147 = bf16[4,64,1024]{2,1,0:T(8,128)(2,1)S(1)} fusion(bf16[1064,4,64]{0,2,1:T(8,128)(2,1)} %bitcast.176, f32[4,1024,1064]{1,2,0:T(8,128)} %get-tuple-element.324, f32[4,1024]{1,0:T(4,128)S(1)} %fusion.146, f32[4,1024]{1,0:T(4,128)S(1)} %get-tuple-element.325), kind=kOutput, calls=%fused_computation.5.clone.1 | convolution fusion | flops 570916864 | bytes 18534400 | tf_op jit(solution)/shard_map/while/body/eval_jaxpr/hqk,khd->qhd/dot_general | solution.py:171
  207.1 7.7 %fusion.145 = (f32[4,1024]{1,0:T(4,128)S(1)}, f32[4,1024,1064]{1,2,0:T(8,128)}) fusion(bf16[1024,4,64]{0,2,1:T(8,128)(2,1)S(1)} %bitcast.173, bf16[1064,4,64]{0,2,1:T(8,128)(2,1)S(1)} %bitcast.171, pred[1024,1064]{0,1:T(8,128)(4,1)S(1)} %get-tuple-element.360), kind=kOutput, calls=%fused_computation.153.clone.1 | convolution fusion | flops 570912768 | bytes 19607552 | tf_op jit(solution)/shard_map/while/body/eval_jaxpr/qhd,khd->hqk/dot_general | solution.py:158
  214.8 8.3 %fusion.146 = f32[4,1024]{1,0:T(4,128)S(1)} fusion(f32[4,1024,1064]{1,2,0:T(8,128)} %get-tuple-element.324, f32[4,1024]{1,0:T(4,128)S(1)} %get-tuple-element.325), kind=kLoop, calls=%fused_computation.4.clone.1 | loop fusion | flops 8712192 | bytes 17465344 | tf_op jit(solution)/shard_map/while/body/eval_jaxpr/reduce_sum | solution.py:168
  223.1 9.3 %fusion.147 = bf16[4,64,1024]{2,1,0:T(8,128)(2,1)S(1)} fusion(bf16[1064,4,64]{0,2,1:T(8,128)(2,1)} %bitcast.176, f32[4,1024,1064]{1,2,0:T(8,128)} %get-tuple-element.324, f32[4,1024]{1,0:T(4,128)S(1)} %fusion.146, f32[4,1024]{1,0:T(4,128)S(1)} %get-tuple-element.325), kind=kOutput, calls=%fused_computation.5.clone.1 | convolution fusion | flops 570916864 | bytes 18534400 | tf_op jit(solution)/shard_map/while/body/eval_jaxpr/hqk,khd->qhd/dot_general | solution.py:171
  233.7 5.0 fusion.79
  240.8 12.8 %fusion.36 = f32[1024,4096]{1,0:T(8,128)} fusion(bf16[1024,4096]{1,0:T(8,128)(2,1)S(1)} %bitcast.197, f32[1024,1024]{0,1:T(8,128)S(1)} %get-tuple-element.213, f32[1024]{0:T(1024)S(1)} %copy-done.31, f32[1024]{0:T(1024)S(1)} %copy-done.25, f32[1024]{0:T(1024)S(1)} %fusion.62, f32[1024]{0:T(1024)S(1)} %broadcast_multiply_fusion), kind=kOutput, calls=%fused_computation.81 | convolution fusion | flops 8595177472 | bytes 29376512 | tf_op jit(solution)/shard_map/dot_general | solution.py:188
  253.5 16.6 %add_convert_fusion.1 = bf16[1024,1024]{0,1:T(8,128)(2,1)} fusion(f32[1024,1024]{0,1:T(8,128)} %copy-done.4, bf16[4096,1024]{1,0:T(8,128)(2,1)} %param.36, f32[1024,4096]{1,0:T(8,128)} %fusion.36), kind=kOutput, calls=%fused_computation.71 | convolution fusion | flops 8629780480 | bytes 31457280 | tf_op jit(solution)/shard_map/dot_general | solution.py:190
  270.1 24.5 %fusion.16.clone.4 = bf16[1024,4096]{1,0:T(8,128)(2,1)S(1)} fusion(f32[1024,4096]{1,0:T(8,128)} %fusion.36, bf16[1024,1024]{1,0:T(8,128)(2,1)} %param.37, bf16[4096,1024]{1,0:T(8,128)(2,1)} %param.36), kind=kOutput, calls=%fused_computation.37.clone.clone.clone.clone.1 | convolution fusion | flops 8690597888 | bytes 35651584 | tf_op jit(solution)/shard_map/rc,fc->rf/dot_general | solution.py:193
  294.6 11.5 %multiply_reduce_fusion.1 = (f32[1024]{0:T(1024)S(1)}, f32[1024,1024]{0,1:T(8,128)S(1)}) fusion(f32[1024,1024]{0,1:T(8,128)S(1)} %copy-done.5, f32[1024]{0:T(1024)S(1)} %copy-done.25, f32[1024]{0:T(1024)S(1)} %broadcast_multiply_fusion, bf16[1024,4096]{1,0:T(8,128)(2,1)} %param.35, bf16[1024,4096]{1,0:T(8,128)(2,1)S(1)} %fusion.16.clone.4), kind=kOutput, calls=%fused_computation.70 | convolution fusion | flops 8594127872 | bytes 25178112 | tf_op jit(solution)/shard_map/rf,cf->rc/dot_general | solution.py:198
  307.8 3.7 fusion.47
  313.1 216.8 %while.29 = (s32[]{:T(128)}, bf16[4,1024,256]{1,2,0:T(8,128)(2,1)}, f32[4,1064,256]{1,2,0:T(8,128)}, f32[4,1064,256]{1,2,0:T(8,128)}, bf16[4,1064,256]{1,2,0:T(8...) while((s32[]{:T(128)}, bf16[4,1024,256]{1,2,0:T(8,128)(2,1)}, ...), condition=%wide.region_16.17_spmd, body=%wide.region_14.16_spmd.sunk | while | flops 2829228032 | bytes 148213904 | solution.py:247
  316.6 8.4 %fusion.158 = f32[4,1024,1064]{1,2,0:T(8,128)} fusion(bf16[1024,4,64]{0,2,1:T(8,128)(2,1)S(1)} %bitcast.163, bf16[1064,4,64]{0,2,1:T(8,128)(2,1)S(1)} %bitcast.172), kind=kOutput, calls=%fused_computation.158.clone.1 | convolution fusion | flops 557842432 | bytes 18501632 | tf_op jit(solution)/shard_map/while/body/eval_jaxpr/qhd,khd->hqk/dot_general | solution.py:219
  326.1 13.1 %multiply_reduce_fusion.4 = (f32[4,1024]{1,0:T(4,128)S(1)}, f32[4,1024,1064]{1,2,0:T(8,128)}) fusion(f32[4,1024,1064]{1,2,0:T(8,128)} %fusion.158, f32[4,1024]{1,0:T(4,128)S(1)} %dynamic-slice_bitcast_fusion.2, bf16[1024,4,64]{0,2,1:T(8,128)(2,1)S(1)} %bitcast.167, bf16[1064,4,64]{0,2,1:T(8,128)(2,1)S(1)} %bitcast.165, ...), kind=kOutput, calls=%fused_computation.15.clone.1 | convolution fusion | flops 579629056 | bytes 37056512 | tf_op jit(solution)/shard_map/while/body/eval_jaxpr/qhd,khd->hqk/dot_general | solution.py:158
  339.2 12.1 %multiply_convert_fusion.8 = bf16[4,1024,1064]{1,2,0:T(8,128)(2,1)S(1)} fusion(f32[4,1024,1064]{1,2,0:T(8,128)} %get-tuple-element.336, f32[4,1024,1064]{1,2,0:T(8,128)} %fusion.158, f32[4,1024]{1,0:T(4,128)S(1)} %get-tuple-element.337), kind=kLoop, calls=%fused_computation.14.clone.1 | loop fusion | flops 13074432 | bytes 43597824 | tf_op jit(solution)/shard_map/while/body/eval_jaxpr/convert_element_type | solution.py:223
  354.3 8.7 %fusion.159 = f32[4,64,1064]{2,1,0:T(8,128)S(1)} fusion(bf16[1024,4,64]{0,2,1:T(8,128)(2,1)S(1)} %bitcast.164, f32[4,1024,1064]{1,2,0:T(8,128)} %get-tuple-element.336), kind=kOutput, calls=%fused_computation.17.clone.1 | convolution fusion | flops 562200576 | bytes 19046400 | tf_op jit(solution)/shard_map/while/body/eval_jaxpr/hqk,qhd->khd/dot_general | solution.py:232
  363.0 2.8 convolution_multiply_fusion.7
  370.7 8.4 %fusion.158 = f32[4,1024,1064]{1,2,0:T(8,128)} fusion(bf16[1024,4,64]{0,2,1:T(8,128)(2,1)S(1)} %bitcast.163, bf16[1064,4,64]{0,2,1:T(8,128)(2,1)S(1)} %bitcast.172), kind=kOutput, calls=%fused_computation.158.clone.1 | convolution fusion | flops 557842432 | bytes 18501632 | tf_op jit(solution)/shard_map/while/body/eval_jaxpr/qhd,khd->hqk/dot_general | solution.py:219
  380.2 13.1 %multiply_reduce_fusion.4 = (f32[4,1024]{1,0:T(4,128)S(1)}, f32[4,1024,1064]{1,2,0:T(8,128)}) fusion(f32[4,1024,1064]{1,2,0:T(8,128)} %fusion.158, f32[4,1024]{1,0:T(4,128)S(1)} %dynamic-slice_bitcast_fusion.2, bf16[1024,4,64]{0,2,1:T(8,128)(2,1)S(1)} %bitcast.167, bf16[1064,4,64]{0,2,1:T(8,128)(2,1)S(1)} %bitcast.165, ...), kind=kOutput, calls=%fused_computation.15.clone.1 | convolution fusion | flops 579629056 | bytes 37056512 | tf_op jit(solution)/shard_map/while/body/eval_jaxpr/qhd,khd->hqk/dot_general | solution.py:158
  393.3 12.1 %multiply_convert_fusion.8 = bf16[4,1024,1064]{1,2,0:T(8,128)(2,1)S(1)} fusion(f32[4,1024,1064]{1,2,0:T(8,128)} %get-tuple-element.336, f32[4,1024,1064]{1,2,0:T(8,128)} %fusion.158, f32[4,1024]{1,0:T(4,128)S(1)} %get-tuple-element.337), kind=kLoop, calls=%fused_computation.14.clone.1 | loop fusion | flops 13074432 | bytes 43597824 | tf_op jit(solution)/shard_map/while/body/eval_jaxpr/convert_element_type | solution.py:223
  408.4 8.7 %fusion.159 = f32[4,64,1064]{2,1,0:T(8,128)S(1)} fusion(bf16[1024,4,64]{0,2,1:T(8,128)(2,1)S(1)} %bitcast.164, f32[4,1024,1064]{1,2,0:T(8,128)} %get-tuple-element.336), kind=kOutput, calls=%fused_computation.17.clone.1 | convolution fusion | flops 562200576 | bytes 19046400 | tf_op jit(solution)/shard_map/while/body/eval_jaxpr/hqk,qhd->khd/dot_general | solution.py:232
  417.2 2.8 convolution_multiply_fusion.7
  424.8 8.4 %fusion.158 = f32[4,1024,1064]{1,2,0:T(8,128)} fusion(bf16[1024,4,64]{0,2,1:T(8,128)(2,1)S(1)} %bitcast.163, bf16[1064,4,64]{0,2,1:T(8,128)(2,1)S(1)} %bitcast.172), kind=kOutput, calls=%fused_computation.158.clone.1 | convolution fusion | flops 557842432 | bytes 18501632 | tf_op jit(solution)/shard_map/while/body/eval_jaxpr/qhd,khd->hqk/dot_general | solution.py:219
  434.3 13.1 %multiply_reduce_fusion.4 = (f32[4,1024]{1,0:T(4,128)S(1)}, f32[4,1024,1064]{1,2,0:T(8,128)}) fusion(f32[4,1024,1064]{1,2,0:T(8,128)} %fusion.158, f32[4,1024]{1,0:T(4,128)S(1)} %dynamic-slice_bitcast_fusion.2, bf16[1024,4,64]{0,2,1:T(8,128)(2,1)S(1)} %bitcast.167, bf16[1064,4,64]{0,2,1:T(8,128)(2,1)S(1)} %bitcast.165, ...), kind=kOutput, calls=%fused_computation.15.clone.1 | convolution fusion | flops 579629056 | bytes 37056512 | tf_op jit(solution)/shard_map/while/body/eval_jaxpr/qhd,khd->hqk/dot_general | solution.py:158
  447.4 12.1 %multiply_convert_fusion.8 = bf16[4,1024,1064]{1,2,0:T(8,128)(2,1)S(1)} fusion(f32[4,1024,1064]{1,2,0:T(8,128)} %get-tuple-element.336, f32[4,1024,1064]{1,2,0:T(8,128)} %fusion.158, f32[4,1024]{1,0:T(4,128)S(1)} %get-tuple-element.337), kind=kLoop, calls=%fused_computation.14.clone.1 | loop fusion | flops 13074432 | bytes 43597824 | tf_op jit(solution)/shard_map/while/body/eval_jaxpr/convert_element_type | solution.py:223
  462.5 8.7 %fusion.159 = f32[4,64,1064]{2,1,0:T(8,128)S(1)} fusion(bf16[1024,4,64]{0,2,1:T(8,128)(2,1)S(1)} %bitcast.164, f32[4,1024,1064]{1,2,0:T(8,128)} %get-tuple-element.336), kind=kOutput, calls=%fused_computation.17.clone.1 | convolution fusion | flops 562200576 | bytes 19046400 | tf_op jit(solution)/shard_map/while/body/eval_jaxpr/hqk,qhd->khd/dot_general | solution.py:232
  471.3 2.8 convolution_multiply_fusion.7
  478.9 8.4 %fusion.158 = f32[4,1024,1064]{1,2,0:T(8,128)} fusion(bf16[1024,4,64]{0,2,1:T(8,128)(2,1)S(1)} %bitcast.163, bf16[1064,4,64]{0,2,1:T(8,128)(2,1)S(1)} %bitcast.172), kind=kOutput, calls=%fused_computation.158.clone.1 | convolution fusion | flops 557842432 | bytes 18501632 | tf_op jit(solution)/shard_map/while/body/eval_jaxpr/qhd,khd->hqk/dot_general | solution.py:219
  488.5 13.1 %multiply_reduce_fusion.4 = (f32[4,1024]{1,0:T(4,128)S(1)}, f32[4,1024,1064]{1,2,0:T(8,128)}) fusion(f32[4,1024,1064]{1,2,0:T(8,128)} %fusion.158, f32[4,1024]{1,0:T(4,128)S(1)} %dynamic-slice_bitcast_fusion.2, bf16[1024,4,64]{0,2,1:T(8,128)(2,1)S(1)} %bitcast.167, bf16[1064,4,64]{0,2,1:T(8,128)(2,1)S(1)} %bitcast.165, ...), kind=kOutput, calls=%fused_computation.15.clone.1 | convolution fusion | flops 579629056 | bytes 37056512 | tf_op jit(solution)/shard_map/while/body/eval_jaxpr/qhd,khd->hqk/dot_general | solution.py:158
  501.5 12.1 %multiply_convert_fusion.8 = bf16[4,1024,1064]{1,2,0:T(8,128)(2,1)S(1)} fusion(f32[4,1024,1064]{1,2,0:T(8,128)} %get-tuple-element.336, f32[4,1024,1064]{1,2,0:T(8,128)} %fusion.158, f32[4,1024]{1,0:T(4,128)S(1)} %get-tuple-element.337), kind=kLoop, calls=%fused_computation.14.clone.1 | loop fusion | flops 13074432 | bytes 43597824 | tf_op jit(solution)/shard_map/while/body/eval_jaxpr/convert_element_type | solution.py:223
  516.6 8.7 %fusion.159 = f32[4,64,1064]{2,1,0:T(8,128)S(1)} fusion(bf16[1024,4,64]{0,2,1:T(8,128)(2,1)S(1)} %bitcast.164, f32[4,1024,1064]{1,2,0:T(8,128)} %get-tuple-element.336), kind=kOutput, calls=%fused_computation.17.clone.1 | convolution fusion | flops 562200576 | bytes 19046400 | tf_op jit(solution)/shard_map/while/body/eval_jaxpr/hqk,qhd->khd/dot_general | solution.py:232
  525.4 2.8 convolution_multiply_fusion.7
  529.9 4.5 slice.73
  537.6 3.9 copy.126
  541.6 10.8 %fusion.31 = (f32[1024]{0:T(1024)S(1)}, f32[1024,1024]{0,1:T(8,128)S(1)}) fusion(bf16[1024,1024]{0,1:T(8,128)(2,1)S(1)} %copy-done.3, f32[1024]{0:T(1024)S(1)} %copy-done.21, f32[1024]{0:T(1024)S(1)} %copy-done.17, bf16[1024,3072]{1,0:T(8,128)(2,1)} %param.31, bf16[1024,1024]{0,1:T(8,128)(2,1)} %bitcast.183, bf16[1024,1024]{0,1:T(8,128)(2,1)} %bitcast.184, ...), kind=kOutput, calls=%fused_computation.65 | convolution fusion | flops 6466567168 | bytes 18886656 | tf_op jit(solution)/shard_map/rk,dk->rd/dot_general | solution.py:263
  558.0 6.0 all-to-all-start.1
  564.0 6.5 add_convert_fusion
  570.5 3.9 copy.127
  576.6 4.2 fusion.83
  580.9 4.7 fusion.57
  586.2 50.5 %all-reduce.5.cloned.1.call-done = f32[16,10,512]{2,1,0:T(8,128)} async-done(((f32[16,10,512]{2,1,0:T(8,128)}), f32[16,10,512]{2,1,0:T(8,128)}) %all-reduce.5.cloned.1.call-update) | async-done | bytes 327696 | tf_op jit(solution)/shard_map/psum | solution.py:295
  639.2 2.7 convolution_bitcast_fusion
  642.7 5.3 copy.129
  (207 shorter events, 97.4 us)
Async XLA Ops:
  7.2 226.5 %copy-start = (bf16[1024,1024]{1,0:T(8,128)(2,1)S(1)}, bf16[1024,1024]{1,0:T(8,128)(2,1)}, u32[]{:S(2)}) copy-start(bf16[1024,1024]{1,0:T(8,128)(2,1)} %param.32) | copy-start | bytes 6291460
  7.2 7.0 %copy-start.32 = (bf16[1024]{0:T(1024)(128)(2,1)S(1)}, bf16[1024]{0:T(1024)(128)(2,1)}, u32[]{:S(2)}) copy-start(bf16[1024]{0:T(1024)(128)(2,1)} %param.30) | copy-start | bytes 6148
  7.2 7.0 %copy-start.33 = (bf16[1024]{0:T(1024)(128)(2,1)S(1)}, bf16[1024]{0:T(1024)(128)(2,1)}, u32[]{:S(2)}) copy-start(bf16[1024]{0:T(1024)(128)(2,1)} %param.29) | copy-start | bytes 6148
  7.2 62.0 %all-reduce.3.cloned.1.call-start = ((), (), s32[]{:S(2)}) async-start(), calls=%async_computation.2 | async-start | bytes 1048576 | tf_op jit(solution)/shard_map/psum | solution.py:91
  14.2 5.5 copy-start.2
  14.2 4.9 copy-start.20
  16.3 2.8 copy-start.16
  18.5 0.6 copy-start.18
  19.1 0.6 copy-start.22
  30.0 2.9 copy-start.30
  30.0 2.9 copy-start.37
  30.0 6.5 copy-start.29
  30.0 6.5 copy-start.26
  36.6 36.0 %copy-start.12 = (f32[16,512]{1,0:T(8,128)}, f32[16,512]{1,0:T(8,128)S(1)}, u32[]{:S(2)}) copy-start(f32[16,512]{1,0:T(8,128)S(1)} %convert_element_type.103) | copy-start | bytes 98308
  79.2 22.4 %all-to-all-start = ((bf16[32,2,1280]{2,1,0:T(2,128)(2,1)}), bf16[32,2,1280]{2,1,0:T(2,128)(2,1)}, u32[]{:S(2)}, u32[]{:S(2)}) async-start(bf16[32,2,1280]{2,1,0:T(2,128)(2,1)} %reshape.376), calls=%async_computation | async-start | bytes 327680 | tf_op jit(solution)/shard_map/all_to_all | solution.py:104
  87.1 7.9 %copy-start.34 = (bf16[1024]{0:T(1024)(128)(2,1)S(1)}, bf16[1024]{0:T(1024)(128)(2,1)}, u32[]{:S(2)}) copy-start(bf16[1024]{0:T(1024)(128)(2,1)} %param.34) | copy-start | bytes 6148
  87.1 8.5 %copy-start.35 = (bf16[1024]{0:T(1024)(128)(2,1)S(1)}, bf16[1024]{0:T(1024)(128)(2,1)}, u32[]{:S(2)}) copy-start(bf16[1024]{0:T(1024)(128)(2,1)} %param.33) | copy-start | bytes 6148
  108.9 6.9 %copy-start.15 = (f32[4,4,1024]{2,1,0:T(4,128)S(1)}, f32[4,4,1024]{2,1,0:T(4,128)}, u32[]{:S(2)}) copy-start(f32[4,4,1024]{2,1,0:T(4,128)} %custom-call) | copy-start | bytes 196612
  233.7 7.1 %slice-start = ((s8[8388608]{0:T(1024)(128)(4,1)}), s8[4194304]{0:T(1024)(128)(4,1)S(1)}, s32[]{:S(2)}) async-start(s8[8388608]{0:T(1024)(128)(4,1)} %bitcast.196), calls=%async_computation.4 | async-start | bytes 8388608
  233.7 7.0 %slice-start.1 = ((s8[8388608]{0:T(1024)(128)(4,1)}), s8[4194304]{0:T(1024)(128)(4,1)S(1)}, s32[]{:S(2)}) async-start(s8[8388608]{0:T(1024)(128)(4,1)} %bitcast.196), calls=%async_computation.5 | async-start | bytes 8388608
  238.7 2.0 copy-start.4
  238.7 2.0 copy-start.25
  238.7 2.0 copy-start.31
  270.1 24.5 %copy-start.5 = (f32[1024,1024]{0,1:T(8,128)S(1)}, f32[1024,1024]{0,1:T(8,128)}, u32[]{:S(2)}) copy-start(f32[1024,1024]{0,1:T(8,128)} %copy-done.4) | copy-start | bytes 12582916
  306.2 1.6 copy-start.9
  307.3 4.2 copy-start.6
  307.4 4.2 copy-start.27
  529.9 5.6 copy-start.11
  535.6 6.0 copy-start.3
  535.6 6.0 copy-start.17
  535.6 6.0 copy-start.21
  541.6 10.8 %copy-start.19 = (f32[1024]{0:T(1024)S(1)}, f32[1024]{0:T(1024)}, u32[]{:S(2)}) copy-start(f32[1024]{0:T(1024)} %copy-done.18) | copy-start | bytes 12292
  541.6 12.8 %copy-start.23 = (f32[1024]{0:T(1024)S(1)}, f32[1024]{0:T(1024)}, u32[]{:S(2)}) copy-start(f32[1024]{0:T(1024)} %copy-done.22) | copy-start | bytes 12292
  552.4 2.0 copy-start.7
  554.4 2.0 copy-start.36
  555.6 8.4 %copy-start.28 = (f32[1024]{0:T(1024)S(1)}, f32[1024]{0:T(1024)}, u32[]{:S(2)}) copy-start(f32[1024]{0:T(1024)} %copy-done.27) | copy-start | bytes 12292
  558.0 18.1 %all-to-all-start.1 = ((f32[32,1,2560]{2,1,0:T(1,128)}), f32[32,1,2560]{2,1,0:T(1,128)S(1)}, u32[]{:S(2)}, u32[]{:S(2)}) async-start(f32[32,1,2560]{2,1,0:T(1,128)} %copy.124), calls=%async_computation.1 | async-start | bytes 655360 | tf_op jit(solution)/shard_map/all_to_all | solution.py:283
  563.9 72.8 %all-reduce.5.cloned.1.call-start = ((), (), s32[]{:S(2)}) async-start(), calls=%async_computation.3 | async-start | bytes 1048576 | tf_op jit(solution)/shard_map/psum | solution.py:295
  570.5 5.6 copy-start.24
  574.5 6.4 copy-start.10
  574.5 6.4 copy-start.13
  580.8 57.8 %copy-start.8 = (bf16[16,128,512]{2,1,0:T(8,128)(2,1)S(1)}, bf16[16,128,512]{2,1,0:T(8,128)(2,1)}, u32[]{:S(2)}) copy-start(bf16[16,128,512]{2,1,0:T(8,128)(2,1)} %param.25) | copy-start | bytes 6291460
  580.8 58.4 %copy-start.14 = (bf16[16,10,128]{2,0,1:T(8,128)(2,1)S(1)}, bf16[16,10,128]{2,0,1:T(8,128)(2,1)}, u32[]{:S(2)}) copy-start(bf16[16,10,128]{2,0,1:T(8,128)(2,1)} %param.24) | copy-start | bytes 122884
  642.0 6.0 copy-start.1
Sparse Core Ops, SparseCore 0:
  10.4 58.8 all-reduce.2
  580.9 55.7 all-reduce.4
where the time goes:
time: 665 us; the launch traced here: 655 us
  matrix products  324 us (49%)
  other arithmetic  112 us (17%)
  local copies, waits for them, and re-layouts  109 us (16%)
  waiting for transfers between devices  84.8 us (13%)
  between operations  15.3 us (2%)
  starting transfers between devices  9.93 us (1%)
    dot_general x8, matrix products, group_scores(): jnp.einsum('qhd,khd->hqk', query_heads, key_heads, preferred_element_type...  83.1 us
    psum x1, waiting for transfers between devices, local(): grad_hidden_table = lax.psum(grad_hidden_part, 'batch')  50.5 us
    convert_element_type x4, other arithmetic, attend_back(): grad_scores = (probs * (grad_probs - inner_sum)).astype(jnp.bfloat16)  48.2 us
    dot_general x4, matrix products, attend(): jnp.einsum('hqk,khd->qhd', probs.astype(jnp.bfloat16), value_heads, prefe...  37.2 us
    dot_general x4, matrix products, attend_back(): jnp.einsum('hqk,qhd->khd', probs.astype(jnp.bfloat16), grad_heads, prefer...  34.9 us
    dot_general x4, matrix products, attend_back(): jnp.einsum('qhd,khd->hqk', grad_heads, value_heads, preferred_element_typ...  33.7 us
    reduce_sum x4, other arithmetic, attend(): total = jnp.sum(lifted, axis=-1, keepdims=True)  33.1 us
    psum x1, waiting for transfers between devices, local(): pre_sum = lax.psum(pre_part, 'batch')  32.6 us
  transfers between devices with their start and end apart: 4, of which 3 were waited for; matrix products, arithmetic and copies ran while one was open for 9% of the time, Pallas kernels for 0%

commit v1 on v0

v1 whole, which is shorter than its diff:
```python
import functools

import jax
import jax.numpy as jnp
from jax import lax
from jax.experimental import pallas as pl
from jax.experimental.pallas import tpu as pltpu
from jax.sharding import PartitionSpec as P


BF = jnp.bfloat16
F = jnp.float32
PAD = 16
NEG = -1e30


def dg(a, b, ca, cb):
    return lax.dot_general(a, b, (((ca,), (cb,)), ((), ())), preferred_element_type=F)


def attn_fwd_kernel(slots, plen, len_ref, q_ref, k_ref, v_ref, pk_ref, pv_ref, o_ref, lse_ref, km):
    rows, pair = q_ref.shape
    blk = rows // slots
    hd = pair // 2
    scale = hd ** -0.5
    single = len_ref[0, 0] > blk
    first = lax.broadcasted_iota(jnp.int32, (1, pair), 1) < hd
    zero = jnp.zeros((), BF)
    k = k_ref[...]
    km[0] = jnp.where(first, k, zero)
    km[1] = jnp.where(first, zero, k)
    vt = v_ref[...].T
    tri = lax.broadcasted_iota(jnp.int32, (blk, blk), 0) <= lax.broadcasted_iota(jnp.int32, (blk, blk), 1)
    live = lax.broadcasted_iota(jnp.int32, (PAD, blk), 0) < plen
    for i in range(slots):
        lo, hi = i * blk, (i + 1) * blk
        q = q_ref[lo:hi, :] * jnp.asarray(scale, BF)
        kp = jnp.where(single, pk_ref[0:PAD, :], pk_ref[i * PAD:(i + 1) * PAD, :])
        vp = jnp.where(single, pv_ref[0:PAD, :], pv_ref[i * PAD:(i + 1) * PAD, :])
        vpt = jnp.concatenate([jnp.where(first, vp, zero), jnp.where(first, zero, vp)], axis=0).T
        sp = dg(jnp.concatenate([jnp.where(first, kp, zero), jnp.where(first, zero, kp)], axis=0), q, 1, 1)
        outs, tops, sums, pps = [], [], [], []
        for h in range(2):
            s_pre = jnp.where(live, sp[h * PAD:(h + 1) * PAD], NEG)
            s_dia = jnp.where(tri, dg(km[h, lo:hi, :], q, 1, 1), NEG)
            top = jnp.maximum(jnp.max(s_dia, axis=0, keepdims=True), jnp.max(s_pre, axis=0, keepdims=True))
            if i:
                s_off = dg(km[h, 0:lo, :], q, 1, 1)
                top = jnp.maximum(top, jnp.where(single, jnp.max(s_off, axis=0, keepdims=True), NEG))
            p_pre = jnp.exp(s_pre - top)
            p_dia = jnp.exp(s_dia - top)
            total = jnp.sum(p_dia, axis=0, keepdims=True) + jnp.sum(p_pre, axis=0, keepdims=True)
            ot = dg(vt[h * hd:(h + 1) * hd, lo:hi], p_dia.astype(BF), 1, 0)
            if i:
                p_off = jnp.exp(s_off - jnp.where(single, top, -NEG))
                total = total + jnp.sum(p_off, axis=0, keepdims=True)
                ot = ot + dg(vt[h * hd:(h + 1) * hd, 0:lo], p_off.astype(BF), 1, 0)
            outs.append(ot)
            tops.append(top)
            sums.append(total)
            pps.append(p_pre.astype(BF))
        pre = dg(vpt, jnp.concatenate(pps, axis=0), 1, 0)
        for h in range(2):
            outs[h] = (outs[h] + pre[h * hd:(h + 1) * hd]) / sums[h]
            lse_ref[0, h:h + 1, lo:hi] = tops[h] + jnp.log(sums[h])
        o_ref[lo:hi, :] = jnp.concatenate(outs, axis=0).T.astype(BF)


def attn_fwd(lengths, qkv, pkv, plen):
    rows = qkv.shape[0]
    width = qkv.shape[1] // 3
    slots = lengths.shape[1]
    pairs = width // 128
    col = lambda off: pl.BlockSpec((rows, 128), lambda h: (0, h + off))
    pcol = lambda off: pl.BlockSpec((slots * PAD, 128), lambda h: (0, h + off))
    return pl.pallas_call(
        functools.partial(attn_fwd_kernel, slots, plen),
        grid=(pairs,),
        in_specs=[pl.BlockSpec(memory_space=pltpu.SMEM), col(0), col(pairs), col(2 * pairs), pcol(0), pcol(pairs)],
        out_specs=[col(0), pl.BlockSpec((1, 2, rows), lambda h: (h, 0, 0))],
        out_shape=[jax.ShapeDtypeStruct((rows, width), BF), jax.ShapeDtypeStruct((pairs, 2, rows), F)],
        scratch_shapes=[pltpu.VMEM((2, rows, 128), BF)],
        compiler_params=pltpu.CompilerParams(vmem_limit_bytes=48 * 2**20),
        name="attend",
    )(lengths, qkv, qkv, qkv, pkv, pkv)


def attn_bwd_kernel(slots, plen, len_ref, q_ref, k_ref, v_ref, pk_ref, pv_ref, o_ref, do_ref, lse_ref,
                    dq_ref, dk_ref, dv_ref, dpk_ref, dpv_ref, km, vm, dka, dva):
    rows, pair = q_ref.shape
    blk = rows // slots
    hd = pair // 2
    scale = hd ** -0.5
    single = len_ref[0, 0] > blk
    first = lax.broadcasted_iota(jnp.int32, (1, pair), 1) < hd
    zero = jnp.zeros((), BF)
    split = lambda a: (jnp.where(first, a, zero), jnp.where(first, zero, a))
    stack = lambda a: jnp.concatenate(split(a), axis=0)
    k = k_ref[...]
    km[0], km[1] = split(k)
    vm[0], vm[1] = split(v_ref[...])
    kt = k.T
    tri = lax.broadcasted_iota(jnp.int32, (blk, blk), 0) <= lax.broadcasted_iota(jnp.int32, (blk, blk), 1)
    live = lax.broadcasted_iota(jnp.int32, (PAD, blk), 0) < plen
    pk_sum = pv_sum = None
    pk_parts, pv_parts = [], []
    for i in range(slots):
        lo, hi = i * blk, (i + 1) * blk
        q = q_ref[lo:hi, :] * jnp.asarray(scale, BF)
        do = do_ref[lo:hi, :]
        kp = stack(jnp.where(single, pk_ref[0:PAD, :], pk_ref[i * PAD:(i + 1) * PAD, :]))
        vp = stack(jnp.where(single, pv_ref[0:PAD, :], pv_ref[i * PAD:(i + 1) * PAD, :]))
        sp = dg(kp, q, 1, 1)
        dpp = dg(vp, do, 1, 1)
        prod = (do.astype(F) * o_ref[lo:hi, :].astype(F)).T
        qs = split(q)
        dos = split(do)
        dqs, dsps = [], []
        dk_new = dv_new = None
        add = lambda a, b: b if a is None else a + b
        pkp = pvp = None
        offk = offv = diak = diav = None
        for h in range(2):
            lse = lse_ref[0, h:h + 1, lo:hi]
            delta = jnp.sum(prod[h * hd:(h + 1) * hd], axis=0, keepdims=True)
            p_pre = jnp.where(live, jnp.exp(sp[h * PAD:(h + 1) * PAD] - lse), 0.0)
            ds_pre = (p_pre * (dpp[h * PAD:(h + 1) * PAD] - delta)).astype(BF)
            p_dia = jnp.where(tri, jnp.exp(dg(km[h, lo:hi, :], q, 1, 1) - lse), 0.0)
            ds_dia = (p_dia * (dg(vm[h, lo:hi, :], do, 1, 1) - delta)).astype(BF)
            diav = add(diav, dg(p_dia.astype(BF), dos[h], 1, 0))
            diak = add(diak, dg(ds_dia, qs[h], 1, 0))
            pvp = add(pvp, dg(p_pre.astype(BF), dos[h], 1, 0))
            pkp = add(pkp, dg(ds_pre, qs[h], 1, 0))
            dqt = dg(kt[h * hd:(h + 1) * hd, lo:hi], ds_dia, 1, 0)
            if i:
                p_off = jnp.exp(dg(km[h, 0:lo, :], q, 1, 1) - jnp.where(single, lse, -NEG))
                ds_off = (p_off * (dg(vm[h, 0:lo, :], do, 1, 1) - delta)).astype(BF)
                offv = add(offv, dg(p_off.astype(BF), dos[h], 1, 0))
                offk = add(offk, dg(ds_off, qs[h], 1, 0))
                dqt = dqt + dg(kt[h * hd:(h + 1) * hd, 0:lo], ds_off, 1, 0)
            dqs.append(dqt)
            dsps.append(ds_pre)
        dqt = jnp.concatenate(dqs, axis=0) + dg(kp.T, jnp.concatenate(dsps, axis=0), 1, 0)
        dq_ref[lo:hi, :] = (dqt.T * scale).astype(BF)
        dka[lo:hi, :] = diak
        dva[lo:hi, :] = diav
        if i:
            dka[0:lo, :] += offk
            dva[0:lo, :] += offv
        pk_parts.append(pkp)
        pv_parts.append(pvp)
    dk_ref[...] = dka[...].astype(BF)
    dv_ref[...] = dva[...].astype(BF)
    for i in range(slots):
        for ref, parts in ((dpk_ref, pk_parts), (dpv_ref, pv_parts)):
            whole = sum(parts) if i == 0 else jnp.zeros_like(parts[0])
            ref[i * PAD:(i + 1) * PAD, :] = jnp.where(single, whole, parts[i])


def attn_bwd(lengths, qkv, pkv, attended, grad_att, lse, plen):
    rows = qkv.shape[0]
    width = qkv.shape[1] // 3
    slots = lengths.shape[1]
    pairs = width // 128
    col = lambda off: pl.BlockSpec((rows, 128), lambda h: (0, h + off))
    pcol = lambda off: pl.BlockSpec((slots * PAD, 128), lambda h: (0, h + off))
    sds = jax.ShapeDtypeStruct
    return pl.pallas_call(
        functools.partial(attn_bwd_kernel, slots, plen),
        grid=(pairs,),
        in_specs=[pl.BlockSpec(memory_space=pltpu.SMEM), col(0), col(pairs), col(2 * pairs), pcol(0), pcol(pairs),
                  col(0), col(0), pl.BlockSpec((1, 2, rows), lambda h: (h, 0, 0))],
        out_specs=[col(0), col(0), col(0), pcol(0), pcol(0)],
        out_shape=[sds((rows, width), BF)] * 3 + [sds((slots * PAD, width), F)] * 2,
        scratch_shapes=[pltpu.VMEM((2, rows, 128), BF)] * 2 + [pltpu.VMEM((rows, 128), F)] * 2,
        compiler_params=pltpu.CompilerParams(vmem_limit_bytes=48 * 2**20),
        name="attend_back",
    )(lengths, qkv, qkv, qkv, pkv, pkv, attended, grad_att, lse)


def layer_norm(values, norm_gain, norm_bias):
    average = jnp.mean(values, axis=-1, keepdims=True)
    centered = values - average
    variance = jnp.mean(centered * centered, axis=-1, keepdims=True)
    return centered * lax.rsqrt(variance + 1e-05) * norm_gain + norm_bias


def gelu_tanh(values):
    return (
        0.5
        * values
        * (1.0 + jnp.tanh(0.7978845608028654 * (values + 0.044715 * values * values * values)))
    )


def pick_sum(selector, values):
    return jnp.sum(jnp.where(selector[:, :, None], values[:, None, :], 0.0), axis=0)


def local(
    tokens,
    lengths,
    task_ids,
    prefix_embed,
    reparam_inner,
    reparam_inner_bias,
    reparam_outer,
    reparam_outer_bias,
    first_gain,
    first_bias,
    input_weight,
    output_weight,
    second_gain,
    second_bias,
    expand_weight,
    contract_weight,
    output_cotangent,
):
    width = tokens.shape[1]
    task_dev = prefix_embed.shape[0]
    prefix_len = prefix_embed.shape[1]
    slot_count = lengths.shape[1]
    task_count = lax.axis_size("task")
    batch_count = lax.axis_size("batch")
    device_count = task_count * batch_count
    pair_cols = reparam_outer.shape[2]
    task_row = lax.axis_index("task")
    device_pos = lax.axis_index(("task", "batch"))
    owner_rows = task_ids // task_dev
    row_match = owner_rows[:, :, None] == jnp.arange(task_count, dtype=jnp.int32)[None, None, :]
    row_task = jnp.sum(jnp.where(row_match, task_ids[:, :, None], 0), axis=1)
    own_tasks = task_row * task_dev + jnp.arange(task_dev, dtype=jnp.int32)
    partner_tasks = jnp.take(row_task, task_row, axis=1)
    partner_pick = partner_tasks[:, None] == own_tasks[None, :]
    pre_part = jnp.einsum(
        "tpd,tdh->tph", prefix_embed, reparam_inner, preferred_element_type=jnp.float32
    )
    pre_sum = lax.psum(pre_part, "batch")
    hidden_full = jnp.tanh(pre_sum + reparam_inner_bias.astype(jnp.float32)[:, None, :])
    hidden_low = hidden_full.astype(jnp.bfloat16)
    kv_cols = (
        jnp.einsum("tph,thc->tpc", hidden_low, reparam_outer, preferred_element_type=jnp.float32)
        + reparam_outer_bias.astype(jnp.float32)[:, None, :]
    ).astype(jnp.bfloat16)
    outgoing = jnp.einsum(
        "et,tpc->epc",
        partner_pick.astype(jnp.bfloat16),
        kv_cols,
        preferred_element_type=jnp.float32,
    ).astype(jnp.bfloat16)
    incoming = lax.all_to_all(
        outgoing.reshape(device_count, prefix_len * pair_cols),
        ("task", "batch"),
        split_axis=0,
        concat_axis=0,
        tiled=True,
    )
    by_row = (
        incoming.reshape(task_count, batch_count, prefix_len, pair_cols)
        .transpose(0, 2, 1, 3)
        .reshape(task_count, prefix_len * 2 * width)
    )
    own_owner = jnp.take(owner_rows, device_pos, axis=0)
    slot_match = own_owner[:, None] == jnp.arange(task_count, dtype=jnp.int32)[None, :]
    slot_pick = slot_match.astype(jnp.bfloat16)
    prefix_kv = (
        jnp.dot(slot_pick, by_row, preferred_element_type=jnp.float32)
        .astype(jnp.bfloat16)
        .reshape(slot_count, prefix_len, 2 * width)
    )
    gain_one = first_gain.astype(jnp.float32)
    bias_one = first_bias.astype(jnp.float32)
    gain_two = second_gain.astype(jnp.float32)
    bias_two = second_bias.astype(jnp.float32)
    residual_in = tokens.astype(jnp.float32)
    normed = layer_norm(residual_in, gain_one, bias_one).astype(jnp.bfloat16)
    projected = jnp.dot(normed, input_weight, preferred_element_type=jnp.float32).astype(
        jnp.bfloat16
    )
    prefix_kv = jnp.pad(prefix_kv, ((0, 0), (0, PAD - prefix_len), (0, 0))).reshape(slot_count * PAD, 2 * width)
    attended, log_totals = attn_fwd(lengths, projected, prefix_kv, prefix_len)
    mid = residual_in + jnp.dot(attended, output_weight, preferred_element_type=jnp.float32)
    normed_two = layer_norm(mid, gain_two, bias_two).astype(jnp.bfloat16)
    hidden_pre = jnp.dot(normed_two, expand_weight, preferred_element_type=jnp.float32)
    activated = gelu_tanh(hidden_pre).astype(jnp.bfloat16)
    output = (mid + jnp.dot(activated, contract_weight, preferred_element_type=jnp.float32)).astype(
        jnp.bfloat16
    )
    grad_act = jnp.einsum(
        "rc,fc->rf", output_cotangent, contract_weight, preferred_element_type=jnp.float32
    )
    unused_gelu, gelu_pull = jax.vjp(gelu_tanh, hidden_pre)
    grad_hidden = gelu_pull(grad_act)[0].astype(jnp.bfloat16)
    grad_normed_two = jnp.einsum(
        "rf,cf->rc", grad_hidden, expand_weight, preferred_element_type=jnp.float32
    )
    unused_norm_two, norm_two_pull = jax.vjp(
        lambda values: layer_norm(values, gain_two, bias_two), mid
    )
    grad_mid = output_cotangent.astype(jnp.float32) + norm_two_pull(grad_normed_two)[0]
    grad_mid_low = grad_mid.astype(jnp.bfloat16)
    grad_attended = jnp.einsum(
        "rc,dc->rd", grad_mid_low, output_weight, preferred_element_type=jnp.float32
    ).astype(jnp.bfloat16)
    grad_q, grad_k, grad_v, grad_pk, grad_pv = attn_bwd(
        lengths, projected, prefix_kv, attended, grad_attended, log_totals, prefix_len
    )
    grad_qkv = jnp.concatenate([grad_q, grad_k, grad_v], axis=1)
    grad_normed = jnp.einsum(
        "rk,dk->rd", grad_qkv, input_weight, preferred_element_type=jnp.float32
    )
    unused_norm_one, norm_one_pull = jax.vjp(
        lambda values: layer_norm(values, gain_one, bias_one), residual_in
    )
    input_grad = (grad_mid + norm_one_pull(grad_normed)[0]).astype(jnp.bfloat16)
    grad_prefix = (
        jnp.concatenate([grad_pk, grad_pv], axis=1)
        .reshape(slot_count, PAD, 2 * width)[:, :prefix_len]
        .reshape(slot_count, prefix_len * 2 * width)
    )
    by_owner = pick_sum(slot_match, grad_prefix)
    outgoing_grad = (
        by_owner.reshape(task_count, prefix_len, batch_count, pair_cols)
        .transpose(0, 2, 1, 3)
        .reshape(device_count, prefix_len * pair_cols)
    )
    incoming_grad = lax.all_to_all(
        outgoing_grad, ("task", "batch"), split_axis=0, concat_axis=0, tiled=True
    )
    grad_cols = pick_sum(partner_pick, incoming_grad).reshape(task_dev, prefix_len, pair_cols)
    grad_table_low = grad_cols.astype(jnp.bfloat16)
    grad_outer_bias = jnp.sum(grad_table_low.astype(jnp.float32), axis=1)
    grad_outer = jnp.einsum(
        "tph,tpc->thc", hidden_low, grad_table_low, preferred_element_type=jnp.float32
    )
    grad_hidden_part = jnp.einsum(
        "tpc,thc->tph", grad_table_low, reparam_outer, preferred_element_type=jnp.float32
    )
    grad_hidden_table = lax.psum(grad_hidden_part, "batch")
    grad_pre = (grad_hidden_table * (1.0 - hidden_full * hidden_full)).astype(jnp.bfloat16)
    grad_inner_bias = jnp.sum(grad_pre.astype(jnp.float32), axis=1)
    grad_inner = jnp.einsum(
        "tpd,tph->tdh", prefix_embed, grad_pre, preferred_element_type=jnp.float32
    )
    grad_embed = jnp.einsum(
        "tph,tdh->tpd", grad_pre, reparam_inner, preferred_element_type=jnp.float32
    )
    return (
        output,
        input_grad,
        grad_embed,
        grad_inner,
        grad_inner_bias,
        grad_outer,
        grad_outer_bias,
    )


def solution(mesh):
    placed = (
        P(("task", "batch"), None),
        P(("task", "batch"), None),
        P(),
        P("task", None, "batch"),
        P("task", "batch", None),
        P("task", None),
        P("task", None, "batch"),
        P("task", "batch"),
        P(),
        P(),
        P(),
        P(),
        P(),
        P(),
        P(),
        P(),
        P(("task", "batch"), None),
    )
    return jax.shard_map(
        local,
        mesh=mesh,
        in_specs=placed,
        out_specs=(
            P(("task", "batch"), None),
            P(("task", "batch"), None),
            P("task", None, "batch"),
            P("task", "batch", None),
            P("task", None),
            P("task", None, "batch"),
            P("task", "batch"),
        ),
        check_vma=False,
    )
```

time: 665 us -> 358 us (0.54)
  matrix products: 324 us -> 118 us
  other arithmetic: 112 us -> 19.5 us
  local copies, waits for them, and re-layouts: 109 us -> 30 us
  Pallas kernels: 0 us -> 68.3 us
  waiting for transfers between devices: 84.8 us -> 94.1 us
    dot_general x28 -> x0, matrix products: 209 us -> none  [the longest x8 83.1 us: group_scores(): jnp.einsum('qhd,khd->hqk', query_heads, key_heads, preferred_element_type...]
    pallas_call x0 -> x2, Pallas kernels: none -> 68.3 us  [the longest x1 39 us: attn_bwd(): pl.pallas_call(functools.partial(attn_bwd_kernel, slots, plen), grid=(pai...]
    convert_element_type x4 -> x0, other arithmetic: 48.2 us -> none  [attend_back(): grad_scores = (probs * (grad_probs - inner_sum)).astype(jnp.bfloat16)]
    reduce_sum x5 -> x0, other arithmetic: 33.2 us -> none  [the longest x4 33.1 us: attend(): total = jnp.sum(lifted, axis=-1, keepdims=True)]
    dynamic_slice x24 -> x0, local copies, waits for them, and re-layouts: 30.4 us -> none  [local(): lax.scan(attend, jnp.float32(0.0), (query_groups, key_groups, value_groups))]
    dynamic_update_slice x12 -> x0, local copies, waits for them, and re-layouts: 12.9 us -> none  [the longest x8 6.68 us: local(): lax.scan(attend, jnp.float32(0.0), (query_groups, key_groups, value_groups))]
    slice x8 -> x0, local copies, waits for them, and re-layouts: 11.6 us -> none  [the longest x1 4.51 us: local(): grad_values_all[prefix_rows:]]
    concatenate x6 -> x0, local copies, waits for them, and re-layouts: 10.9 us -> none  [the longest x3 5.77 us: local(): jnp.concatenate([prefix_kv[:, :, :width].reshape(slot_count * prefix_len,...]
  transfers between devices with their start and end apart: 4 -> 4, of which waited for: 3 -> 4; matrix products, arithmetic and copies ran while one was open for 9% -> 12% of each run, Pallas kernels for 0% -> 0%
where the time goes in v1:
time: 358 us; the launch traced here: 352 us
  matrix products  118 us (33%)
  waiting for transfers between devices  94.1 us (26%)
  Pallas kernels  68.3 us (19%)
  local copies, waits for them, and re-layouts  30 us (8%)
  other arithmetic  19.5 us (5%)
  between operations  14.8 us (4%)
  starting transfers between devices  6.77 us (2%)
    psum x1, waiting for transfers between devices, local(): grad_hidden_table = lax.psum(grad_hidden_part, 'batch')  51.2 us
    pallas_call x1, Pallas kernels, attn_bwd(): pl.pallas_call(functools.partial(attn_bwd_kernel, slots, plen), grid=(pai...  39 us
    psum x1, waiting for transfers between devices, local(): pre_sum = lax.psum(pre_part, 'batch')  38.4 us
    pallas_call x1, Pallas kernels, attn_fwd(): pl.pallas_call(functools.partial(attn_fwd_kernel, slots, plen), grid=(pai...  29.3 us
    unnamed x69, local copies, waits for them, and re-layouts  27.3 us
    dot_general x1, matrix products, local(): jnp.einsum('rc,fc->rf', output_cotangent, contract_weight, preferred_elem...  27 us
    dot_general x1, matrix products, local(): jnp.dot(activated, contract_weight, preferred_element_type=jnp.float32)  16.8 us
    dot_general x1, matrix products, local(): jnp.einsum('rf,cf->rc', grad_hidden, expand_weight, preferred_element_typ...  14.8 us
  transfers between devices with their start and end apart: 4, of which 4 were waited for; matrix products, arithmetic and copies ran while one was open for 12% of the time, Pallas kernels for 0%

profile of v1, /device:TPU:0, one launch (start us, length us, event | category | flops | bytes accessed | tf_op | source)
XLA Modules:
  0.0 351.9 jit_solution(11855546239940804049)
XLA Ops:
  7.2 0.0 all-reduce.4.cloned.1.call-start
  7.2 2.9 fusion.46
  10.2 0.0 all-reduce.4.cloned.1.call-update
  10.2 3.9 %copy.82 = bf16[1024,1024]{0,1:T(8,128)(2,1)} copy(bf16[1024,1024]{1,0:T(8,128)(2,1)} %param.17) | data formatting | bytes 4194304 | tf_op args[0]
  14.2 2.0 convert_reduce_fusion
  16.2 2.2 fusion.19
  18.4 0.6 copy-done.14
  19.0 12.3 %convolution_convert_fusion.1.q_ref.k_ref.v_ref = bf16[1024,3072]{1,0:T(8,128)(2,1)} fusion(bf16[1024,3072]{1,0:T(8,128)(2,1)} %param.27, bf16[1024,1024]{0,1:T(8,128)(2,1)} %copy.82, f32[1024]{0:T(1024)S(1)} %convert_element_type.84, f32[1024]{0:T(1024)S(1)} %convert_element_type.83, f32[1024]{0:T(1024)S(1)} %fusion.52, f32[1024]{0:T(1024)S(1)} %broadcast_multiply_fusion.1), kind=kOutput, calls=%fused_computation.29 | convolution fusion | flops 6451888128 | bytes 14696448 | tf_op jit(solution)/shard_map/dot_general | solution.py:277
  31.4 38.4 %all-reduce.4.cloned.1.call-done = f32[16,10,512]{2,1,0:T(8,128)} async-done(((f32[16,10,512]{2,1,0:T(8,128)}), f32[16,10,512]{2,1,0:T(8,128)}) %all-reduce.4.cloned.1.call-update) | async-done | bytes 327696 | tf_op jit(solution)/shard_map/psum | solution.py:238
  69.8 3.0 fusion.41
  72.8 0.3 convolution_convert_fusion.2
  73.2 0.1 copy.85
  73.3 0.1 all_to_all.16
  73.4 0.5 broadcast.276
  73.9 1.6 reduce.2
  75.5 0.7 reshape.234
  76.2 4.1 %all-to-all-start = ((bf16[32,2,1280]{2,1,0:T(2,128)(2,1)}), bf16[32,2,1280]{2,1,0:T(2,128)(2,1)S(1)}, u32[]{:S(2)}, u32[]{:S(2)}) async-start(bf16[32,2,1280]{2,1,0:T(2,128)(2,1)} %reshape.234), calls=%async_computation | async-start | bytes 327680 | tf_op jit(solution)/shard_map/all_to_all | solution.py:251
  80.3 0.1 broadcast_compare_fusion
  80.4 4.0 %copy.89 = bf16[1024,1024]{0,1:T(8,128)(2,1)} copy(bf16[1024,1024]{1,0:T(8,128)(2,1)} %param.33) | data formatting | bytes 4194304 | tf_op args[16]
  84.4 0.7 copy.90
  85.1 0.2 select_reduce_fusion.3
  85.3 0.1 iota_compare_fusion.1
  85.3 3.5 all-to-all-done
  88.8 0.1 reshape.235
  88.9 0.1 copy.99
  89.0 0.3 convolution_convert_fusion
  89.3 0.1 reshape.163
  89.5 29.3 %attend.1 = (bf16[1024,1024]{1,0:T(8,128)(2,1)S(1)}, f32[8,2,1024]{2,1,0:T(2,128)S(1)}) custom-call(s32[1,4]{1,0:T(1,128)S(1)} %copy-done.2, bf16[1024,3072]{1,0:T(8,128)(2,1)} %convolution_convert_fusion.1.q_ref.k_ref.v_ref, bf16[1024,3072]{1,0:T(8,128)(2,1)} %convolution_convert_fusion.1.q_ref.k_ref.v_ref, ...), custom_call_target="tpu_custom_call" | custom-call | tf_op jit(solution)/shard_map/attend/pallas_call | solution.py:76
  118.8 2.6 fusion.67
  121.5 0.5 multiply_reduce_fusion.1
  122.0 1.5 copy-done.5
  123.5 0.8 slice-done.1
  124.3 12.4 %fusion.27 = f32[1024,4096]{1,0:T(8,128)} fusion(bf16[1024,4096]{1,0:T(8,128)(2,1)S(1)} %bitcast.68, f32[1024,1024]{0,1:T(8,128)S(1)} %get-tuple-element.83, f32[1024]{0:T(1024)S(1)} %convert_element_type.94, f32[1024]{0:T(1024)S(1)} %convert_element_type.93, f32[1024]{0:T(1024)S(1)} %fusion.53, f32[1024]{0:T(1024)S(1)} %broadcast_multiply_fusion), kind=kOutput, calls=%fused_computation.45 | convolution fusion | flops 8595177472 | bytes 29376512 | tf_op jit(solution)/shard_map/dot_general | solution.py:284
  136.8 16.8 %add_convert_fusion.1 = bf16[1024,1024]{0,1:T(8,128)(2,1)} fusion(f32[1024,1024]{0,1:T(8,128)} %copy-done.5, bf16[4096,1024]{1,0:T(8,128)(2,1)} %param.32, f32[1024,4096]{1,0:T(8,128)} %fusion.27), kind=kOutput, calls=%fused_computation.39 | convolution fusion | flops 8629780480 | bytes 31457280 | tf_op jit(solution)/shard_map/dot_general | solution.py:286
  153.6 27.0 %fusion.8.clone.4 = bf16[1024,4096]{1,0:T(8,128)(2,1)} fusion(f32[1024,4096]{1,0:T(8,128)} %fusion.27, bf16[1024,1024]{1,0:T(8,128)(2,1)} %param.33, bf16[4096,1024]{1,0:T(8,128)(2,1)} %param.32), kind=kOutput, calls=%fused_computation.8.clone.clone.clone.clone.1 | convolution fusion | flops 8690597888 | bytes 35651584 | tf_op jit(solution)/shard_map/rc,fc->rf/dot_general | solution.py:289
  180.5 3.9 %copy.93 = bf16[1024,1024]{1,0:T(8,128)(2,1)} copy(bf16[1024,1024]{0,1:T(8,128)(2,1)} %add_convert_fusion.1) | data formatting | bytes 4194304
  184.5 14.8 %multiply_reduce_fusion = (f32[1024]{0:T(1024)S(1)}, f32[1024,1024]{0,1:T(8,128)S(1)}) fusion(f32[1024,1024]{0,1:T(8,128)} %copy-done.5, f32[1024]{0:T(1024)S(1)} %convert_element_type.93, f32[1024]{0:T(1024)S(1)} %broadcast_multiply_fusion, bf16[1024,4096]{1,0:T(8,128)(2,1)} %param.31, bf16[1024,4096]{1,0:T(8,128)(2,1)} %fusion.8.clone.4), kind=kOutput, calls=%fused_computation.38 | convolution fusion | flops 8594127872 | bytes 25178112 | tf_op jit(solution)/shard_map/rf,cf->rc/dot_general | solution.py:294
  199.3 1.0 fusion.66
  200.4 0.5 copy-done.9
  200.9 3.8 %fusion.38.do_ref = bf16[1024,1024]{1,0:T(8,128)(2,1)} fusion(bf16[1024,1024]{1,0:T(8,128)(2,1)S(1)} %copy-done, f32[1024,1024]{0,1:T(8,128)S(1)} %get-tuple-element.81, bf16[1024,1024]{0,1:T(8,128)(2,1)S(1)} %copy-done.9, f32[1024]{0:T(1024)S(1)} %negate_multiply_fusion.1), kind=kOutput, calls=%fused_computation.55 | convolution fusion | flops 2152726528 | bytes 10489856 | tf_op jit(solution)/shard_map/rc,dc->rd/dot_general | solution.py:302
  204.7 39.0 %attend_back.1 = (bf16[1024,1024]{1,0:T(8,128)(2,1)S(1)}, bf16[1024,1024]{1,0:T(8,128)(2,1)S(1)}, bf16[1024,1024]{1,0:T(8,128)(2,1)}, f32[64,1024]{1,0:T(8,128)S(1)}, f32[64,1024]{1,0:T(8,128)S(1)}) custom-call(s32[1,4]{1,0:T(1,128)S(1)} %copy-done.2, bf16[1024,3072]{1,0:T(8,128)(2,1)} %convolution_convert_fusion.1.q_ref.k_ref.v_ref, ...), custom_call_target="tpu_custom_call" | custom-call | tf_op jit(solution)/shard_map/attend_back/pallas_call | solution.py:168
  243.8 8.4 %fusion.23 = (f32[1024]{0:T(1024)S(1)}, f32[1024,1024]{0,1:T(8,128)S(1)}) fusion(bf16[1024,1024]{0,1:T(8,128)(2,1)S(1)} %copy-done.4, f32[1024]{0:T(1024)S(1)} %convert_element_type.83, f32[1024]{0:T(1024)S(1)} %broadcast_multiply_fusion.1, bf16[1024,3072]{1,0:T(8,128)(2,1)S(1)} %bitcast.70, bf16[1024,1024]{1,0:T(8,128)(2,1)} %get-tuple-element.18, ...), kind=kOutput, calls=%fused_computation.35 | convolution fusion | flops 6466567168 | bytes 18886656 | tf_op jit(solution)/shard_map/rk,dk->rd/dot_general | solution.py:309
  252.2 1.2 fusion.42
  253.4 0.7 copy-done.8
  254.2 0.2 copy.100
  254.4 0.4 select_reduce_fusion.1
  254.8 0.1 copy.110
  254.9 1.1 copy.91
  255.9 2.6 all-to-all-start.1
  258.5 0.0 all-reduce.6.cloned.1.call-start
  258.6 7.2 %add_convert_fusion = bf16[1024,1024]{0,1:T(8,128)(2,1)} fusion(f32[1024,1024]{0,1:T(8,128)} %copy-done.7, bf16[1024,1024]{0,1:T(8,128)(2,1)} %copy.89, f32[1024]{0:T(1024)S(1)} %negate_multiply_fusion, f32[1024]{0:T(1024)S(1)} %negate_multiply_fusion.1, f32[1024]{0:T(1024)S(1)} %multiply_multiply_fusion.2, f32[1024]{0:T(1024)S(1)} %broadcast_multiply_fusion.1, ...), kind=kLoop, calls=%fused_computation.36 | loop fusion | flops 13631488 | bytes 14704640 | tf_op jit(solution)/shard_map/convert_element_type | solution.py:315
  265.8 3.9 %copy.94 = bf16[1024,1024]{1,0:T(8,128)(2,1)} copy(bf16[1024,1024]{0,1:T(8,128)(2,1)} %add_convert_fusion) | data formatting | bytes 4194304
  269.8 0.9 all-to-all-done.1
  270.7 0.4 select_reduce_fusion
  271.2 0.1 convert_element_type.104
  271.2 4.2 %fusion.70 = f32[16,10,512]{2,1,0:T(8,128)} fusion(bf16[16,10,256]{2,1,0:T(8,128)(2,1)S(1)} %convert_element_type.104, bf16[16,512,256]{2,1,0:T(8,128)(2,1)} %param.23), kind=kOutput, calls=%fused_computation.113 | convolution fusion | flops 41943040 | bytes 4603904 | tf_op jit(solution)/shard_map/tpc,thc->tph/dot_general | solution.py:336
  275.5 4.7 %fusion.48 = f32[16,512,256]{2,1,0:T(8,128)} fusion(bf16[16,10,256]{2,1,0:T(8,128)(2,1)S(1)} %convert_element_type.104, f32[16,10,512]{2,1,0:T(8,128)S(1)} %copy-done.10, f32[16,512]{1,0:T(8,128)S(1)} %copy-done.12), kind=kOutput, calls=%fused_computation.74 | convolution fusion | flops 42106880 | bytes 8830976 | tf_op jit(solution)/shard_map/tph,tpc->thc/dot_general | solution.py:333
  280.2 0.7 convert_reduce_fusion.2
  280.9 51.2 %all-reduce.6.cloned.1.call-done = f32[16,10,512]{2,1,0:T(8,128)} async-done(((f32[16,10,512]{2,1,0:T(8,128)}), f32[16,10,512]{2,1,0:T(8,128)}) %all-reduce.6.cloned.1.call-update) | async-done | bytes 327696 | tf_op jit(solution)/shard_map/psum | solution.py:339
  332.1 1.9 convert_reduce_fusion.1
  333.9 2.2 fusion.71
  336.2 2.7 convolution_bitcast_fusion
  338.9 0.7 copy.95
  339.6 5.3 %copy.96 = f32[16,128,512]{2,1,0:T(8,128)} copy(f32[16,128,512]{1,2,0:T(8,128)} %convolution_bitcast_fusion) | data formatting | bytes 8388608
  (77 shorter events, 0.4 us)
Async XLA Ops:
  7.2 111.6 %copy-start = (bf16[1024,1024]{1,0:T(8,128)(2,1)S(1)}, bf16[1024,1024]{1,0:T(8,128)(2,1)}, u32[]{:S(2)}) copy-start(bf16[1024,1024]{1,0:T(8,128)(2,1)} %param.28) | copy-start | bytes 6291460
  7.2 7.0 %copy-start.20 = (bf16[1024]{0:T(1024)(128)(2,1)S(1)}, bf16[1024]{0:T(1024)(128)(2,1)}, u32[]{:S(2)}) copy-start(bf16[1024]{0:T(1024)(128)(2,1)} %param.26) | copy-start | bytes 6148
  7.2 7.0 %copy-start.21 = (bf16[1024]{0:T(1024)(128)(2,1)S(1)}, bf16[1024]{0:T(1024)(128)(2,1)}, u32[]{:S(2)}) copy-start(bf16[1024]{0:T(1024)(128)(2,1)} %param.25) | copy-start | bytes 6148
  7.2 62.6 %all-reduce.4.cloned.1.call-start = ((), (), s32[]{:S(2)}) async-start(), calls=%async_computation.2 | async-start | bytes 1048576 | tf_op jit(solution)/shard_map/psum | solution.py:238
  10.2 8.7 %copy-start.19 = (s32[32,4]{0,1:T(4,128)S(1)}, s32[32,4]{0,1:T(4,128)}, u32[]{:S(2)}) copy-start(s32[32,4]{0,1:T(4,128)} %param.19) | copy-start | bytes 1540
  18.3 0.6 copy-start.14
  19.0 12.3 %copy-start.18 = (bf16[16,256]{1,0:T(8,128)(2,1)S(1)}, bf16[16,256]{1,0:T(8,128)(2,1)}, u32[]{:S(2)}) copy-start(bf16[16,256]{1,0:T(8,128)(2,1)} %param.24) | copy-start | bytes 24580
  19.0 12.3 %copy-start.17 = (bf16[16,512]{1,0:T(8,128)(2,1)S(1)}, bf16[16,512]{1,0:T(8,128)(2,1)}, u32[]{:S(2)}) copy-start(bf16[16,512]{1,0:T(8,128)(2,1)} %param.22) | copy-start | bytes 49156
  31.3 49.1 %copy-start.22 = (bf16[1024]{0:T(1024)(128)(2,1)S(1)}, bf16[1024]{0:T(1024)(128)(2,1)}, u32[]{:S(2)}) copy-start(bf16[1024]{0:T(1024)(128)(2,1)} %param.30) | copy-start | bytes 6148
  31.3 49.1 %copy-start.23 = (bf16[1024]{0:T(1024)(128)(2,1)S(1)}, bf16[1024]{0:T(1024)(128)(2,1)}, u32[]{:S(2)}) copy-start(bf16[1024]{0:T(1024)(128)(2,1)} %param.29) | copy-start | bytes 6148
  31.4 41.8 %copy-start.11 = (f32[16,512]{1,0:T(8,128)}, f32[16,512]{1,0:T(8,128)S(1)}, u32[]{:S(2)}) copy-start(f32[16,512]{1,0:T(8,128)S(1)} %convert_element_type.87) | copy-start | bytes 98308
  73.3 16.2 %copy-start.2 = (s32[1,4]{1,0:T(1,128)S(1)}, s32[1,4]{1,0:T(1,128)}, u32[]{:S(2)}) copy-start(s32[1,4]{1,0:T(1,128)} %len_ref.3) | copy-start | bytes 52
  76.2 12.6 %all-to-all-start = ((bf16[32,2,1280]{2,1,0:T(2,128)(2,1)}), bf16[32,2,1280]{2,1,0:T(2,128)(2,1)S(1)}, u32[]{:S(2)}, u32[]{:S(2)}) async-start(bf16[32,2,1280]{2,1,0:T(2,128)(2,1)} %reshape.234), calls=%async_computation | async-start | bytes 327680 | tf_op jit(solution)/shard_map/all_to_all | solution.py:251
  89.5 29.3 %copy-start.3 = (bf16[1024,1024]{0,1:T(8,128)(2,1)S(1)}, bf16[1024,1024]{0,1:T(8,128)(2,1)}, u32[]{:S(2)}) copy-start(bf16[1024,1024]{0,1:T(8,128)(2,1)} %copy.82) | copy-start | bytes 6291460
  118.8 2.7 copy-start.1
  118.8 4.7 %slice-start = ((s8[8388608]{0:T(1024)(128)(4,1)}), s8[4194304]{0:T(1024)(128)(4,1)S(1)}, s32[]{:S(2)}) async-start(s8[8388608]{0:T(1024)(128)(4,1)} %bitcast.67), calls=%async_computation.4 | async-start | bytes 8388608
  118.8 5.5 %slice-start.1 = ((s8[8388608]{0:T(1024)(128)(4,1)}), s8[4194304]{0:T(1024)(128)(4,1)S(1)}, s32[]{:S(2)}) async-start(s8[8388608]{0:T(1024)(128)(4,1)} %bitcast.67), calls=%async_computation.5 | async-start | bytes 8388608
  121.5 2.1 copy-start.5
  184.5 14.8 %copy-start.6 = (f32[1024,1024]{0,1:T(8,128)S(1)}, f32[1024,1024]{0,1:T(8,128)}, u32[]{:S(2)}) copy-start(f32[1024,1024]{0,1:T(8,128)} %copy-done.5) | copy-start | bytes 12582916
  199.3 1.6 copy-start.9
  199.3 44.4 %slice-start.2 = ((s8[6291456]{0:T(1024)(128)(4,1)}), s8[4194304]{0:T(1024)(128)(4,1)S(1)}, s32[]{:S(2)}) async-start(s8[6291456]{0:T(1024)(128)(4,1)} %bitcast.69), calls=%async_computation.6 | async-start | bytes 8388608
  200.4 4.3 %copy-start.7 = (f32[1024,1024]{0,1:T(8,128)}, f32[1024,1024]{0,1:T(8,128)S(1)}, u32[]{:S(2)}) copy-start(f32[1024,1024]{0,1:T(8,128)S(1)} %get-tuple-element.81) | copy-start | bytes 12582916
  200.9 42.8 %slice-start.3 = ((s8[6291456]{0:T(1024)(128)(4,1)}), s8[2097152]{0:T(1024)(128)(4,1)S(1)}, s32[]{:S(2)}) async-start(s8[6291456]{0:T(1024)(128)(4,1)} %bitcast.69), calls=%async_computation.7 | async-start | bytes 4194304
  204.7 39.1 %copy-start.4 = (bf16[1024,1024]{0,1:T(8,128)(2,1)S(1)}, bf16[1024,1024]{0,1:T(8,128)(2,1)}, u32[]{:S(2)}) copy-start(bf16[1024,1024]{0,1:T(8,128)(2,1)} %copy.82) | copy-start | bytes 6291460
  243.8 8.4 %copy-start.15 = (f32[1024]{0:T(1024)S(1)}, f32[1024]{0:T(1024)}, u32[]{:S(2)}) copy-start(f32[1024]{0:T(1024)} %copy-done.14) | copy-start | bytes 12292
  252.1 2.0 copy-start.8
  255.9 14.7 %all-to-all-start.1 = ((f32[32,1,2560]{2,1,0:T(1,128)}), f32[32,1,2560]{2,1,0:T(1,128)S(1)}, u32[]{:S(2)}, u32[]{:S(2)}) async-start(f32[32,1,2560]{2,1,0:T(1,128)} %copy.91), calls=%async_computation.1 | async-start | bytes 655360 | tf_op jit(solution)/shard_map/all_to_all | solution.py:327
  258.5 73.5 %all-reduce.6.cloned.1.call-start = ((), (), s32[]{:S(2)}) async-start(), calls=%async_computation.3 | async-start | bytes 1048576 | tf_op jit(solution)/shard_map/psum | solution.py:339
  265.8 4.9 %copy-start.16 = (pred[32,16]{1,0:T(8,128)(4,1)S(1)}, pred[32,16]{1,0:T(8,128)(4,1)}, u32[]{:S(2)}) copy-start(pred[32,16]{1,0:T(8,128)(4,1)} %copy.90) | copy-start | bytes 1540
  269.8 5.7 %copy-start.10 = (f32[16,10,512]{2,1,0:T(8,128)S(1)}, f32[16,10,512]{2,1,0:T(8,128)}, u32[]{:S(2)}) copy-start(f32[16,10,512]{2,1,0:T(8,128)} %all-reduce.4.cloned.1.call-done) | copy-start | bytes 983044
  269.8 5.7 %copy-start.12 = (f32[16,512]{1,0:T(8,128)S(1)}, f32[16,512]{1,0:T(8,128)}, u32[]{:S(2)}) copy-start(f32[16,512]{1,0:T(8,128)} %copy-done.11) | copy-start | bytes 98308
  275.5 60.7 %copy-start.13 = (bf16[16,10,128]{2,0,1:T(8,128)(2,1)S(1)}, bf16[16,10,128]{2,0,1:T(8,128)(2,1)}, u32[]{:S(2)}) copy-start(bf16[16,10,128]{2,0,1:T(8,128)(2,1)} %param.20) | copy-start | bytes 122884
Sparse Core Ops, SparseCore 0:
  10.9 58.8 all-reduce.3
  275.6 56.4 all-reduce.5
